TPU v7x, 128 devices: a whole 4x4x4 slice. The times are simulated.
128 devices in a mesh: bulk: 32 (over z, x_hi, y), grp: 4 (over x_lo, core).
Axes of the slice: x: 4 (x_hi: 2, x_lo: 2; x = x_hi * 2 + x_lo), y: 4, z: 4, core: 2. Of those that a mesh axis runs over, the one named last changes fastest.
Arguments:
- positions: float32 [3, 3145728], P(None, ('bulk', 'grp')), may hold values from -1 to 1
- normals: float32 [3, 3145728], P(None, ('bulk', 'grp')), may hold values from -6 to 6
- strength: float32 [3145728], P(('bulk', 'grp')), may hold values from -6 to 6
- near_index: int32 [24576, 6, 2], P(('bulk', 'grp')), may hold values from 0 to 191
- near_count: int32 [24576, 6], P(('bulk', 'grp')), may hold values from 0 to 2
Outputs:
- potential: float32 [3145728], P(('bulk', 'grp'))
Inputs may be any that keep to these rules, and one draw needn't show every extreme that they name: `near_index`: indexes a block among the 192 blocks of the round's partner device.
All inputs are finite; a program needn't handle non-finite values.
Results may differ from a plain program's by a relative error of at most 0.0003.
Values sent between devices are 32-bit elements; how exact they have to be, the bound alone decides.
No kernel may reach another device: no remote copies, remote signals or barrier semaphores. Data moves between devices by JAX's collectives and lax.ppermute only.
A program may use at most 64 MiB of HBM per device.

v0:
```python
import functools
import math

import jax
import jax.numpy as jnp
from jax import lax
from jax.experimental import pallas as pl
from jax.experimental.pallas import tpu as pltpu
from jax.sharding import PartitionSpec as P

DELTA2 = 0.05
BLK = 128
U = 52
KF = 48
STEPS = 4
PAD = 128
OWN = 6


def from_partner(x, axis, stride):
    return lax.ppermute(x, axis, [(i, i ^ 1 << stride) for i in range(lax.axis_size(axis))])


def split3(v):
    h = v.astype(jnp.bfloat16).astype(jnp.float32)
    r = v - h
    m = r.astype(jnp.bfloat16).astype(jnp.float32)
    return h, m, r - m


def row(msg, c, nb, b):
    return jnp.broadcast_to(msg[pl.ds(c * nb + b, 1), :], (8, BLK))


def target_features(msg, nb, b, sub):
    x, y, z = row(msg, 0, nb, b), row(msg, 1, nb, b), row(msg, 2, nb, b)
    k = jnp.where(sub < 3, sub, sub - 3)
    v = jnp.where(k == 0, x, jnp.where(k == 1, y, z))
    h, m, l = split3(jnp.where(sub < 6, v, x * x + y * y + z * z + DELTA2))
    for_dist = jnp.where(sub < 3, -2.0, 0.0)
    six = jnp.where(sub == 6, 1.0, 0.0)
    seven = jnp.where(sub == 7, -1.0, 0.0)
    is_six, mid = sub == 6, (sub >= 3) & (sub < 6)
    h2, m2 = h * for_dist, m * for_dist
    dh = h2 + six
    dmh, dmm = jnp.where(is_six, h, m2), jnp.where(is_six, m, m2)
    dl = l * (for_dist + six)
    nh, nm, nl = jnp.where(mid, h, seven), jnp.where(mid, m, 0.0), jnp.where(mid, l, 0.0)
    dist = jnp.concatenate([dh, dh, dh, dmh, dmm, dl], axis=0)
    num = jnp.concatenate([nh, nh, nh, nm, nm, nl], axis=0)
    return jnp.concatenate([dist, num], axis=1).astype(jnp.bfloat16)


def source_features(stage, step, j, sub):
    h, m, l = split3(stage[pl.ds(j, 8, stride=step), :])
    hu = jnp.where(sub < 6, h, 1.0)
    mu = jnp.where(sub < 6, m, 1.0)
    return jnp.concatenate([h, m, l, hu, mu, hu], axis=0)


def phase_kernel(nb, chain, carry_in, carry_out, last, lists_in, *refs):
    own = not carry_in
    n = len(chain)
    n_msg = n - (1 if carry_in else 0)
    msgs, refs = refs[:n_msg], refs[n_msg:]
    if own:
        out, tgt, refs = refs[0], refs[1], refs[2:]
    else:
        before, tgt, src_in, out, refs = refs[0], refs[1], refs[2], refs[3], refs[4:]
    if carry_out:
        src_out, refs = refs[0], refs[1:]
    acc, stage, lists, sem, kept = refs[0], refs[1], refs[2], refs[3], list(refs[4:])
    copy = pltpu.make_async_copy(lists_in, lists, sem)
    copy.start()
    src = ([src_in] if carry_in else []) + kept + ([src_out] if carry_out else [])
    width = 2 * nb + PAD
    sub = lax.broadcasted_iota(jnp.int32, (8, BLK), 0)

    if own:
        acc[...] = jnp.zeros_like(acc)
        tgt[nb] = jnp.zeros((KF, 2 * BLK), jnp.bfloat16)
    else:
        acc[pl.ds(0, nb)] = before[...]

    step = nb // STEPS

    def make(k, i):
        msg = msgs[k - (1 if carry_in else 0)]
        for g in range(0, step, 8):
            rows = [msg[pl.ds(pl.multiple_of(c * nb + i * step + g, 8), 8), :] for c in range(6)]
            x, y, z, u, v, w = rows
            rows += [x * x + y * y + z * z, x * u + y * v + z * w]
            for c, value in enumerate(rows):
                stage[pl.ds(c * step + g, 8), :] = value
        for j in range(step):
            b = i * step + j
            f = source_features(stage, step, j, sub)
            src[k][pl.ds(pl.multiple_of(b * BLK, BLK), BLK), :KF] = f.astype(jnp.bfloat16).T
            if chain[k] == OWN:
                tgt[b] = target_features(msg, nb, b, sub)

    def tiles(slots, between):
        codes, prods = [], []
        for k, p in slots:
            codes.append(lists[chain[k] * width + p])
        for (k, _), code in zip(slots, codes):
            a = src[k][pl.ds(pl.multiple_of((code & 255) * BLK, BLK), BLK), :KF]
            prods.append(jnp.dot(a, tgt[code >> 12], preferred_element_type=jnp.float32))
        between()
        for code, p in zip(codes, prods):
            s = lax.rsqrt(p[:, :BLK])
            w = p[:, BLK:] * (s * (s * s))
            acc[code >> 12] += jnp.sum(w.reshape(16, 8, BLK), axis=0)

    if own:

        def first(i, _):
            make(0, i)
            return 0

        lax.fori_loop(0, STEPS, first, 0)

    copy.wait()
    sizes = [lists[7 * width + i] for i in chain]
    for k in range(1, n):

        def both(i, _, k=k):
            each = step if chain[k - 1] == OWN else U
            tiles([(k - 1, i * each + u) for u in range(each)], lambda: make(k, i))
            return 0

        lax.fori_loop(0, STEPS, both, 0)

    groups = [([k for k in range(n - 1) if chain[k] != OWN], STEPS * U)]
    groups += [] if carry_out else [([n - 1], 0)]
    for group, done in groups:
        if not group:
            continue
        each = U // len(group)
        todo = jnp.int32(0)
        for k in group:
            todo = jnp.maximum(todo, (sizes[k] - done + each - 1) // each)

        def rest(i, _, group=group, each=each, done=done):
            at = done + i * each
            tiles([(k, jnp.minimum(at + u, width - 1)) for k in group for u in range(each)], lambda: None)
            return 0

        lax.fori_loop(0, todo, rest, 0)

    if last:

        def finish(i, _):
            out[pl.ds(pl.multiple_of(i * 8, 8), 8), :] = jnp.sum(acc[pl.ds(i * 8, 8)], axis=1)
            return 0

        lax.fori_loop(0, nb // 8, finish, 0, unroll=4)
    else:
        out[...] = acc[pl.ds(0, nb)]


def phase(name, chain, lists, msgs, before, carry_out):
    nb = msgs[0].shape[0] // 6
    carry_in = len(before) > 0
    last = not carry_out
    near, vmem = pl.BlockSpec(memory_space=pl.ANY), pl.BlockSpec(memory_space=pltpu.VMEM)
    args = [lists, *msgs, *before]
    shapes = [jax.ShapeDtypeStruct((nb, BLK) if last else (nb, 8, BLK), jnp.float32)]
    if not carry_in:
        shapes.append(jax.ShapeDtypeStruct((nb + 1, KF, 2 * BLK), jnp.bfloat16))
    if carry_out:
        shapes.append(jax.ShapeDtypeStruct((nb * BLK, BLK), jnp.bfloat16))
    kept = len(chain) - (1 if carry_in else 0) - (1 if carry_out else 0)
    return pl.pallas_call(
        functools.partial(phase_kernel, nb, tuple(chain), carry_in, carry_out, last),
        out_shape=shapes,
        in_specs=[near] + [vmem] * (len(args) - 1),
        out_specs=[vmem] * len(shapes),
        scratch_shapes=[pltpu.VMEM((nb + 1, 8, BLK), jnp.float32), pltpu.VMEM((8 * nb // STEPS, BLK), jnp.float32)]
        + [pltpu.SMEM(lists.shape, jnp.int32), pltpu.SemaphoreType.DMA]
        + [pltpu.VMEM((nb * BLK, BLK), jnp.bfloat16)] * kept,
        compiler_params=pltpu.CompilerParams(vmem_limit_bytes=26 << 20),
        cost_estimate=pl.CostEstimate(
            flops=len(chain) * 2_000_000_000, bytes_accessed=len(chain) * 1_000_000, transcendentals=0
        ),
        name=name,
    )(*args)


def start_kernel(nb, rounds, *refs):
    outside, (msg, lists), inside, sems = refs[:5], refs[5:7], refs[7:12], refs[12]
    copies = [pltpu.make_async_copy(o, i, sems.at[n]) for n, (o, i) in enumerate(zip(outside, inside))]
    for copy in copies[::-1]:
        copy.start()
    pos, nrm, dens, index, count = inside

    def plane(i, _):
        for j in range(8):
            b = i * 8 + j
            at = pl.ds(pl.multiple_of(b * BLK, BLK), BLK)
            msg[pl.ds(b, 3, stride=nb), :] = pos[:, at]
            q = dens[pl.ds(b, 1), :] * (1.0 / (4.0 * math.pi))
            msg[pl.ds(3 * nb + b, 3, stride=nb), :] = nrm[:, at] * q
        return 0

    copies[4].wait()
    copies[3].wait()
    width = 2 * nb + PAD
    slots = index.shape[1]
    c = count[...]
    t_row = lax.broadcasted_iota(jnp.int32, (nb, nb), 0)
    t_col = lax.broadcasted_iota(jnp.int32, (nb, nb), 1)
    earlier = jnp.where(t_row < t_col, 1.0, 0.0).astype(jnp.bfloat16)
    pad = jnp.zeros((16 - rounds, nb), jnp.float32)
    cf = jnp.concatenate([c.astype(jnp.float32), pad], axis=0)
    before = jnp.dot(cf.astype(jnp.bfloat16), earlier, preferred_element_type=jnp.float32)
    size = jnp.sum(cf, axis=1, keepdims=True)
    place = lax.broadcasted_iota(jnp.int32, (1, width), 1)
    spot = lax.broadcasted_iota(jnp.int32, (width, nb), 0).astype(jnp.float32)
    t = lax.broadcasted_iota(jnp.int32, (1, nb), 1).astype(jnp.float32)
    rest = jnp.zeros((14, nb), jnp.float32)
    rows = []
    for r in range(rounds):
        both = jnp.zeros((16, width), jnp.float32)
        for s in range(slots):
            at = jnp.where(cf[r:r + 1] > s, before[r:r + 1] + s, -1.0)
            hot = jnp.where(spot == at, 1.0, 0.0).astype(jnp.bfloat16)
            code = jnp.concatenate([index[r, pl.ds(s, 1), :].astype(jnp.float32), t, rest], axis=0)
            both += lax.dot_general(
                code.astype(jnp.bfloat16), hot, (((1,), (1,)), ((), ())), preferred_element_type=jnp.float32
            )
        row = (both[1:2] * 4096.0 + both[0:1]).astype(jnp.int32)
        rows.append(jnp.where(place.astype(jnp.float32) < size[r:r + 1], row, nb << 12))
    rows.append(jnp.where(place < nb, (place << 12) + place, nb << 12))
    sub = lax.broadcasted_iota(jnp.int32, (16, BLK), 0)
    lane = lax.broadcasted_iota(jnp.int32, (16, BLK), 1)
    sizes = jnp.sum(jnp.where(sub == lane, size, 0.0), axis=0, keepdims=True)
    sizes = jnp.where(lane[:1] == rounds, float(nb), sizes).astype(jnp.int32)
    parts = width // BLK
    for i, row in enumerate(rows):
        for q in range(parts):
            lists[pl.ds(i * parts + q, 1), :] = row[:, q * BLK:(q + 1) * BLK]
    lists[pl.ds(len(rows) * parts, 1), :] = sizes
    for copy in copies[:3]:
        copy.wait()
    lax.fori_loop(0, nb // 8, plane, 0)


def start(positions, normals, strength, near_index, near_count):
    nb, rounds, slots = near_index.shape
    rows = (rounds + 2) * (slots * nb + PAD) // BLK
    vmem = pl.BlockSpec(memory_space=pltpu.VMEM)
    index = near_index.transpose(1, 2, 0)
    args = [positions, normals, strength.reshape(nb, BLK), index, near_count.T]
    msg, lists = pl.pallas_call(
        functools.partial(start_kernel, nb, rounds),
        out_shape=[
            jax.ShapeDtypeStruct((6 * nb, BLK), jnp.float32),
            jax.ShapeDtypeStruct((rows, BLK), jnp.int32),
        ],
        in_specs=[pl.BlockSpec(memory_space=pltpu.HBM)] * 5,
        out_specs=[vmem] * 2,
        scratch_shapes=[pltpu.VMEM(a.shape, a.dtype) for a in args] + [pltpu.SemaphoreType.DMA((5,))],
        compiler_params=pltpu.CompilerParams(vmem_limit_bytes=24 << 20),
        name="start",
    )(*[pltpu.with_memory_space_constraint(a, pltpu.HBM) for a in args])
    return msg, lists.reshape(-1)


def shards(positions, normals, strength, near_index, near_count):
    mine, lists = start(positions, normals, strength, near_index, near_count)
    top_bit = lax.axis_size("bulk").bit_length() - 2
    plan = [("grp", 0), ("grp", 1), ("bulk", 0), ("bulk", 1), ("bulk", 2), ("bulk", top_bit)]
    far = [from_partner(mine, axis, bit) for axis, bit in plan]
    a, tgt, held = phase("own_core", [OWN, 0], lists, [mine, far[0]], [], True)
    b, held = phase("mid", [0, 2, 1, 5], lists, [far[2], far[1], far[5]], [a, tgt, held], True)
    (c,) = phase("end", [5, 3, 4], lists, [far[3], far[4]], [b, tgt, held], False)
    return c.reshape(-1)


def solution(mesh):
    in_specs = (
        P(None, ("bulk", "grp")),
        P(None, ("bulk", "grp")),
        P(("bulk", "grp")),
        P(("bulk", "grp"), None, None),
        P(("bulk", "grp"), None),
    )
    out_specs = P(("bulk", "grp"))
    return jax.shard_map(shards, mesh=mesh, in_specs=in_specs, out_specs=out_specs, check_vma=False)
```

profile of v0, /device:TPU:1, one launch (start us, length us, event | category | flops | bytes accessed | tf_op | source)
XLA Modules:
  0.0 54.0 jit_solution(5003846817037770231)
XLA Ops:
  0.0 2.5 %start.1 = (f32[1152,128]{1,0:T(8,128)S(1)}, s32[32,128]{1,0:T(8,128)S(1)}) custom-call(f32[3,24576]{1,0:T(4,128)} %refs_0_.1, f32[3,24576]{1,0:T(4,128)} %refs_1_.1, f32[192,128]{1,0:T(8,128)} %bitcast.8, s32[6,2,192]{2,1,0:T(2,128)} %bitcast.9, s32[6,192]{1,0:T(8,128)} %bitcast.10), custom_call_target="tpu_custom_call" | custom-call | tf_op jit(solution)/shard_map/start/pallas_call | solution.py:255
  2.5 1.5 %collective-permute-start.5 = (f32[1152,128]{1,0:T(8,128)S(1)}, f32[1152,128]{1,0:T(8,128)S(1)}, u32[]{:S(2)}, u32[]{:S(2)}) collective-permute-start(f32[1152,128]{1,0:T(8,128)S(1)} %get-tuple-element.13.refs_0_), channel_id=1, source_target_pairs={{0,1},{1,0},{2,3},{3,2},{4,5},{5,4},{6,7},{7,6},{8,9},{9,8},{10,11... | collective-permute-start | bytes 1769480 | tf_op jit(solution)/shard_map/ppermute | solution.py:21
  4.0 1.4 %collective-permute-start.2 = (f32[1152,128]{1,0:T(8,128)S(1)}, f32[1152,128]{1,0:T(8,128)S(1)}, u32[]{:S(2)}, u32[]{:S(2)}) collective-permute-start(f32[1152,128]{1,0:T(8,128)S(1)} %get-tuple-element.13.refs_0_), channel_id=1, source_target_pairs={{0,4},{4,0},{8,12},{12,8},{16,20},{20,16},{24,28},{28,24},{32,36},... | collective-permute-start | bytes 1769480 | tf_op jit(solution)/shard_map/ppermute | solution.py:21
  5.4 1.2 %collective-permute-start.3 = (f32[1152,128]{1,0:T(8,128)S(1)}, f32[1152,128]{1,0:T(8,128)S(1)}, u32[]{:S(2)}, u32[]{:S(2)}) collective-permute-start(f32[1152,128]{1,0:T(8,128)S(1)} %get-tuple-element.13.refs_0_), channel_id=1, source_target_pairs={{0,2},{1,3},{2,0},{3,1},{4,6},{5,7},{6,4},{7,5},{8,10},{9,11},{10,... | collective-permute-start | bytes 1769480 | tf_op jit(solution)/shard_map/ppermute | solution.py:21
  6.6 3.6 %collective-permute-start.4 = (f32[1152,128]{1,0:T(8,128)S(1)}, f32[1152,128]{1,0:T(8,128)S(1)}, u32[]{:S(2)}, u32[]{:S(2)}) collective-permute-start(f32[1152,128]{1,0:T(8,128)S(1)} %get-tuple-element.13.refs_0_), channel_id=1, source_target_pairs={{0,64},{4,68},{8,72},{12,76},{16,80},{20,84},{24,88},{28,92},{32,9... | collective-permute-start | bytes 1769480 | tf_op jit(solution)/shard_map/ppermute | solution.py:21
  10.2 2.6 %collective-permute-start = (f32[1152,128]{1,0:T(8,128)S(1)}, f32[1152,128]{1,0:T(8,128)S(1)}, u32[]{:S(2)}, u32[]{:S(2)}) collective-permute-start(f32[1152,128]{1,0:T(8,128)S(1)} %get-tuple-element.13.refs_0_), channel_id=1, source_target_pairs={{0,8},{4,12},{8,0},{12,4},{16,24},{20,28},{24,16},{28,20},{32,40},... | collective-permute-start | bytes 1769480 | tf_op jit(solution)/shard_map/ppermute | solution.py:21
  12.8 0.0 collective-permute-done.5.refs_1_
  12.8 2.5 %collective-permute-start.1 = (f32[1152,128]{1,0:T(8,128)S(1)}, f32[1152,128]{1,0:T(8,128)S(1)}, u32[]{:S(2)}, u32[]{:S(2)}) collective-permute-start(f32[1152,128]{1,0:T(8,128)S(1)} %get-tuple-element.13.refs_0_), channel_id=1, source_target_pairs={{0,16},{4,20},{8,24},{12,28},{16,0},{20,4},{24,8},{28,12},{32,48},... | collective-permute-start | bytes 1769480 | tf_op jit(solution)/shard_map/ppermute | solution.py:21
  15.3 7.1 %own_core.1 = (f32[192,8,128]{2,1,0:T(8,128)S(1)}, bf16[193,48,256]{2,1,0:T(8,128)(2,1)S(1)}, bf16[24576,128]{1,0:T(8,128)(2,1)S(1)}) custom-call(s32[4096]{0:T(1024)S(1)} %bitcast.5, f32[1152,128]{1,0:T(8,128)S(1)} %get-tuple-element.13.refs_0_, f32[1152,128]{1,0:T(8,128)S(1)} %collective-permute-done.5.refs_1_), custom_call_target="tpu_custom_call" | custom-call | flops 4000000000 | bytes 2000000 | tf_op jit(solution)/shard_map/own_core/pallas_call | solution.py:174
  22.4 0.0 collective-permute-done.2.refs_0_
  22.4 0.0 collective-permute-done.3.refs_1_
  22.4 0.9 %collective-permute-done.4.refs_2_ = f32[1152,128]{1,0:T(8,128)S(1)} collective-permute-done((f32[1152,128]{1,0:T(8,128)S(1)}, f32[1152,128]{1,0:T(8,128)S(1)}, u32[]{:S(2)}, u32[]{:S(2)}) %collective-permute-start.4) | collective-permute-done | bytes 589856 | tf_op jit(solution)/shard_map/ppermute | solution.py:21
  23.3 15.6 %mid.1 = (f32[192,8,128]{2,1,0:T(8,128)S(1)}, bf16[24576,128]{1,0:T(8,128)(2,1)S(1)}) custom-call(s32[4096]{0:T(1024)S(1)} %bitcast.6, f32[1152,128]{1,0:T(8,128)S(1)} %collective-permute-done.2.refs_0_, f32[1152,128]{1,0:T(8,128)S(1)} %collective-permute-done.3.refs_1_, f32[1152,128]{1,0:T(8,128)S(1)} %collective-permute-done.4.refs_2_, ...), custom_call_target="tpu_custom_call" | custom-call | flops 8000000000 | bytes 4000000 | tf_op jit(solution)/shard_map/mid/pallas_call | solution.py:174
  38.9 0.0 collective-permute-done.refs_0_
  38.9 0.0 collective-permute-done.1.refs_1_
  38.9 15.1 %end.1 = f32[192,128]{1,0:T(8,128)} custom-call(s32[4096]{0:T(1024)S(1)} %bitcast.7, f32[1152,128]{1,0:T(8,128)S(1)} %collective-permute-done.refs_0_, f32[1152,128]{1,0:T(8,128)S(1)} %collective-permute-done.1.refs_1_, f32[192,8,128]{2,1,0:T(8,128)S(1)} %get-tuple-element.17.refs_2_, bf16[193,48,256]{2,1,0:T(8,128)(2,1)S(1)} %get-tuple-element.15.refs_4_.refs_3_, ...), custom_call_target="tpu_custom_call" | custom-call | flops 6000000000 | bytes 3000000 | tf_op jit(solution)/shard_map/end/pallas_call | solution.py:174
Async XLA Ops:
  2.5 10.3 %collective-permute-start.5 = (f32[1152,128]{1,0:T(8,128)S(1)}, f32[1152,128]{1,0:T(8,128)S(1)}, u32[]{:S(2)}, u32[]{:S(2)}) collective-permute-start(f32[1152,128]{1,0:T(8,128)S(1)} %get-tuple-element.13.refs_0_), channel_id=1, source_target_pairs={{0,1},{1,0},{2,3},{3,2},{4,5},{5,4},{6,7},{7,6},{8,9},{9,8},{10,11... | collective-permute-start | bytes 1769480 | tf_op jit(solution)/shard_map/ppermute | solution.py:21
  4.0 18.4 %collective-permute-start.2 = (f32[1152,128]{1,0:T(8,128)S(1)}, f32[1152,128]{1,0:T(8,128)S(1)}, u32[]{:S(2)}, u32[]{:S(2)}) collective-permute-start(f32[1152,128]{1,0:T(8,128)S(1)} %get-tuple-element.13.refs_0_), channel_id=1, source_target_pairs={{0,4},{4,0},{8,12},{12,8},{16,20},{20,16},{24,28},{28,24},{32,36},... | collective-permute-start | bytes 1769480 | tf_op jit(solution)/shard_map/ppermute | solution.py:21
  5.4 17.0 %collective-permute-start.3 = (f32[1152,128]{1,0:T(8,128)S(1)}, f32[1152,128]{1,0:T(8,128)S(1)}, u32[]{:S(2)}, u32[]{:S(2)}) collective-permute-start(f32[1152,128]{1,0:T(8,128)S(1)} %get-tuple-element.13.refs_0_), channel_id=1, source_target_pairs={{0,2},{1,3},{2,0},{3,1},{4,6},{5,7},{6,4},{7,5},{8,10},{9,11},{10,... | collective-permute-start | bytes 1769480 | tf_op jit(solution)/shard_map/ppermute | solution.py:21
  6.6 16.7 %collective-permute-start.4 = (f32[1152,128]{1,0:T(8,128)S(1)}, f32[1152,128]{1,0:T(8,128)S(1)}, u32[]{:S(2)}, u32[]{:S(2)}) collective-permute-start(f32[1152,128]{1,0:T(8,128)S(1)} %get-tuple-element.13.refs_0_), channel_id=1, source_target_pairs={{0,64},{4,68},{8,72},{12,76},{16,80},{20,84},{24,88},{28,92},{32,9... | collective-permute-start | bytes 1769480 | tf_op jit(solution)/shard_map/ppermute | solution.py:21
  10.2 28.7 %collective-permute-start = (f32[1152,128]{1,0:T(8,128)S(1)}, f32[1152,128]{1,0:T(8,128)S(1)}, u32[]{:S(2)}, u32[]{:S(2)}) collective-permute-start(f32[1152,128]{1,0:T(8,128)S(1)} %get-tuple-element.13.refs_0_), channel_id=1, source_target_pairs={{0,8},{4,12},{8,0},{12,4},{16,24},{20,28},{24,16},{28,20},{32,40},... | collective-permute-start | bytes 1769480 | tf_op jit(solution)/shard_map/ppermute | solution.py:21
  12.8 26.1 %collective-permute-start.1 = (f32[1152,128]{1,0:T(8,128)S(1)}, f32[1152,128]{1,0:T(8,128)S(1)}, u32[]{:S(2)}, u32[]{:S(2)}) collective-permute-start(f32[1152,128]{1,0:T(8,128)S(1)} %get-tuple-element.13.refs_0_), channel_id=1, source_target_pairs={{0,16},{4,20},{8,24},{12,28},{16,0},{20,4},{24,8},{28,12},{32,48},... | collective-permute-start | bytes 1769480 | tf_op jit(solution)/shard_map/ppermute | solution.py:21
where the time goes:
time: 54.8 us; the launch traced here: 54 us
  Pallas kernels  40.3 us (74%)
  starting transfers between devices  12.8 us (23%)
  waiting for transfers between devices  0.87 us (2%)
    pallas_call x3, Pallas kernels, phase(): pl.pallas_call(functools.partial(phase_kernel, nb, tuple(chain), carry_in...  37.8 us
    ppermute x6, starting transfers between devices, from_partner(): lax.ppermute(x, axis, [(i, i ^ 1 << stride) for i in range(lax.axis_size(...  12.8 us
    pallas_call x1, Pallas kernels, start(): pl.pallas_call(functools.partial(start_kernel, nb, rounds), out_shape=[ja...  2.48 us
  transfers between devices with their start and end apart: 6, of which 1 were waited for; matrix products, arithmetic and copies ran while one was open for 0% of the time, Pallas kernels for 42%

commit v1 on v0

--- a/solution.py
+++ b/solution.py
@@ -243,7 +243,7 @@
     lists[pl.ds(len(rows) * parts, 1), :] = sizes
     for copy in copies[:3]:
         copy.wait()
-    lax.fori_loop(0, nb // 8, plane, 0)
+    lax.fori_loop(0, nb // 8, plane, 0, unroll=4)
 
 
 def start(positions, normals, strength, near_index, near_count):

time: 54.8 us -> 54.8 us (level)
  the two profiles are of different devices: /device:TPU:1 before, /device:TPU:0 now
where the time goes in v1:
time: 54.8 us; the launch traced here: 54.7 us
  Pallas kernels  41.3 us (75%)
  starting transfers between devices  12.8 us (23%)
  waiting for transfers between devices  0.58 us (1%)
    pallas_call x3, Pallas kernels, phase(): pl.pallas_call(functools.partial(phase_kernel, nb, tuple(chain), carry_in...  38.8 us
    ppermute x6, starting transfers between devices, from_partner(): lax.ppermute(x, axis, [(i, i ^ 1 << stride) for i in range(lax.axis_size(...  12.8 us
    pallas_call x1, Pallas kernels, start(): pl.pallas_call(functools.partial(start_kernel, nb, rounds), out_shape=[ja...  2.43 us
  transfers between devices with their start and end apart: 6, of which 1 were waited for; matrix products, arithmetic and copies ran while one was open for 0% of the time, Pallas kernels for 42%

profile of v1, /device:TPU:0, one launch (start us, length us, event | category | flops | bytes accessed | tf_op | source)
XLA Modules:
  0.0 54.7 jit_solution(12300941662076040462)
XLA Ops:
  0.0 2.4 %start.1 = (f32[1152,128]{1,0:T(8,128)S(1)}, s32[32,128]{1,0:T(8,128)S(1)}) custom-call(f32[3,24576]{1,0:T(4,128)} %refs_0_.1, f32[3,24576]{1,0:T(4,128)} %refs_1_.1, f32[192,128]{1,0:T(8,128)} %bitcast.8, s32[6,2,192]{2,1,0:T(2,128)} %bitcast.9, s32[6,192]{1,0:T(8,128)} %bitcast.10), custom_call_target="tpu_custom_call" | custom-call | tf_op jit(solution)/shard_map/start/pallas_call | solution.py:255
  2.4 0.1 collective-permute-start.5
  2.5 1.7 %collective-permute-start.2 = (f32[1152,128]{1,0:T(8,128)S(1)}, f32[1152,128]{1,0:T(8,128)S(1)}, u32[]{:S(2)}, u32[]{:S(2)}) collective-permute-start(f32[1152,128]{1,0:T(8,128)S(1)} %get-tuple-element.13.refs_0_), channel_id=1, source_target_pairs={{0,4},{4,0},{8,12},{12,8},{16,20},{20,16},{24,28},{28,24},{32,36},... | collective-permute-start | bytes 1769480 | tf_op jit(solution)/shard_map/ppermute | solution.py:21
  4.3 1.5 %collective-permute-start.3 = (f32[1152,128]{1,0:T(8,128)S(1)}, f32[1152,128]{1,0:T(8,128)S(1)}, u32[]{:S(2)}, u32[]{:S(2)}) collective-permute-start(f32[1152,128]{1,0:T(8,128)S(1)} %get-tuple-element.13.refs_0_), channel_id=1, source_target_pairs={{0,2},{1,3},{2,0},{3,1},{4,6},{5,7},{6,4},{7,5},{8,10},{9,11},{10,... | collective-permute-start | bytes 1769480 | tf_op jit(solution)/shard_map/ppermute | solution.py:21
  5.8 3.9 %collective-permute-start.4 = (f32[1152,128]{1,0:T(8,128)S(1)}, f32[1152,128]{1,0:T(8,128)S(1)}, u32[]{:S(2)}, u32[]{:S(2)}) collective-permute-start(f32[1152,128]{1,0:T(8,128)S(1)} %get-tuple-element.13.refs_0_), channel_id=1, source_target_pairs={{0,64},{4,68},{8,72},{12,76},{16,80},{20,84},{24,88},{28,92},{32,9... | collective-permute-start | bytes 1769480 | tf_op jit(solution)/shard_map/ppermute | solution.py:21
  9.6 2.9 %collective-permute-start = (f32[1152,128]{1,0:T(8,128)S(1)}, f32[1152,128]{1,0:T(8,128)S(1)}, u32[]{:S(2)}, u32[]{:S(2)}) collective-permute-start(f32[1152,128]{1,0:T(8,128)S(1)} %get-tuple-element.13.refs_0_), channel_id=1, source_target_pairs={{0,8},{4,12},{8,0},{12,4},{16,24},{20,28},{24,16},{28,20},{32,40},... | collective-permute-start | bytes 1769480 | tf_op jit(solution)/shard_map/ppermute | solution.py:21
  12.5 0.0 collective-permute-done.5.refs_1_
  12.5 2.7 %collective-permute-start.1 = (f32[1152,128]{1,0:T(8,128)S(1)}, f32[1152,128]{1,0:T(8,128)S(1)}, u32[]{:S(2)}, u32[]{:S(2)}) collective-permute-start(f32[1152,128]{1,0:T(8,128)S(1)} %get-tuple-element.13.refs_0_), channel_id=1, source_target_pairs={{0,16},{4,20},{8,24},{12,28},{16,0},{20,4},{24,8},{28,12},{32,48},... | collective-permute-start | bytes 1769480 | tf_op jit(solution)/shard_map/ppermute | solution.py:21
  15.3 7.1 %own_core.1 = (f32[192,8,128]{2,1,0:T(8,128)S(1)}, bf16[193,48,256]{2,1,0:T(8,128)(2,1)S(1)}, bf16[24576,128]{1,0:T(8,128)(2,1)S(1)}) custom-call(s32[4096]{0:T(1024)S(1)} %bitcast.5, f32[1152,128]{1,0:T(8,128)S(1)} %get-tuple-element.13.refs_0_, f32[1152,128]{1,0:T(8,128)S(1)} %collective-permute-done.5.refs_1_), custom_call_target="tpu_custom_call" | custom-call | flops 4000000000 | bytes 2000000 | tf_op jit(solution)/shard_map/own_core/pallas_call | solution.py:174
  22.4 0.0 collective-permute-done.2.refs_0_
  22.4 0.0 collective-permute-done.3.refs_1_
  22.4 0.6 %collective-permute-done.4.refs_2_ = f32[1152,128]{1,0:T(8,128)S(1)} collective-permute-done((f32[1152,128]{1,0:T(8,128)S(1)}, f32[1152,128]{1,0:T(8,128)S(1)}, u32[]{:S(2)}, u32[]{:S(2)}) %collective-permute-start.4) | collective-permute-done | bytes 589856 | tf_op jit(solution)/shard_map/ppermute | solution.py:21
  23.0 15.6 %mid.1 = (f32[192,8,128]{2,1,0:T(8,128)S(1)}, bf16[24576,128]{1,0:T(8,128)(2,1)S(1)}) custom-call(s32[4096]{0:T(1024)S(1)} %bitcast.6, f32[1152,128]{1,0:T(8,128)S(1)} %collective-permute-done.2.refs_0_, f32[1152,128]{1,0:T(8,128)S(1)} %collective-permute-done.3.refs_1_, f32[1152,128]{1,0:T(8,128)S(1)} %collective-permute-done.4.refs_2_, ...), custom_call_target="tpu_custom_call" | custom-call | flops 8000000000 | bytes 4000000 | tf_op jit(solution)/shard_map/mid/pallas_call | solution.py:174
  38.6 0.0 collective-permute-done.refs_0_
  38.6 0.0 collective-permute-done.1.refs_1_
  38.6 16.1 %end.1 = f32[192,128]{1,0:T(8,128)} custom-call(s32[4096]{0:T(1024)S(1)} %bitcast.7, f32[1152,128]{1,0:T(8,128)S(1)} %collective-permute-done.refs_0_, f32[1152,128]{1,0:T(8,128)S(1)} %collective-permute-done.1.refs_1_, f32[192,8,128]{2,1,0:T(8,128)S(1)} %get-tuple-element.17.refs_2_, bf16[193,48,256]{2,1,0:T(8,128)(2,1)S(1)} %get-tuple-element.15.refs_4_.refs_3_, ...), custom_call_target="tpu_custom_call" | custom-call | flops 6000000000 | bytes 3000000 | tf_op jit(solution)/shard_map/end/pallas_call | solution.py:174
Async XLA Ops:
  2.4 10.1 %collective-permute-start.5 = (f32[1152,128]{1,0:T(8,128)S(1)}, f32[1152,128]{1,0:T(8,128)S(1)}, u32[]{:S(2)}, u32[]{:S(2)}) collective-permute-start(f32[1152,128]{1,0:T(8,128)S(1)} %get-tuple-element.13.refs_0_), channel_id=1, source_target_pairs={{0,1},{1,0},{2,3},{3,2},{4,5},{5,4},{6,7},{7,6},{8,9},{9,8},{10,11... | collective-permute-start | bytes 1769480 | tf_op jit(solution)/shard_map/ppermute | solution.py:21
  2.5 19.9 %collective-permute-start.2 = (f32[1152,128]{1,0:T(8,128)S(1)}, f32[1152,128]{1,0:T(8,128)S(1)}, u32[]{:S(2)}, u32[]{:S(2)}) collective-permute-start(f32[1152,128]{1,0:T(8,128)S(1)} %get-tuple-element.13.refs_0_), channel_id=1, source_target_pairs={{0,4},{4,0},{8,12},{12,8},{16,20},{20,16},{24,28},{28,24},{32,36},... | collective-permute-start | bytes 1769480 | tf_op jit(solution)/shard_map/ppermute | solution.py:21
  4.3 18.2 %collective-permute-start.3 = (f32[1152,128]{1,0:T(8,128)S(1)}, f32[1152,128]{1,0:T(8,128)S(1)}, u32[]{:S(2)}, u32[]{:S(2)}) collective-permute-start(f32[1152,128]{1,0:T(8,128)S(1)} %get-tuple-element.13.refs_0_), channel_id=1, source_target_pairs={{0,2},{1,3},{2,0},{3,1},{4,6},{5,7},{6,4},{7,5},{8,10},{9,11},{10,... | collective-permute-start | bytes 1769480 | tf_op jit(solution)/shard_map/ppermute | solution.py:21
  5.8 17.2 %collective-permute-start.4 = (f32[1152,128]{1,0:T(8,128)S(1)}, f32[1152,128]{1,0:T(8,128)S(1)}, u32[]{:S(2)}, u32[]{:S(2)}) collective-permute-start(f32[1152,128]{1,0:T(8,128)S(1)} %get-tuple-element.13.refs_0_), channel_id=1, source_target_pairs={{0,64},{4,68},{8,72},{12,76},{16,80},{20,84},{24,88},{28,92},{32,9... | collective-permute-start | bytes 1769480 | tf_op jit(solution)/shard_map/ppermute | solution.py:21
  9.6 29.0 %collective-permute-start = (f32[1152,128]{1,0:T(8,128)S(1)}, f32[1152,128]{1,0:T(8,128)S(1)}, u32[]{:S(2)}, u32[]{:S(2)}) collective-permute-start(f32[1152,128]{1,0:T(8,128)S(1)} %get-tuple-element.13.refs_0_), channel_id=1, source_target_pairs={{0,8},{4,12},{8,0},{12,4},{16,24},{20,28},{24,16},{28,20},{32,40},... | collective-permute-start | bytes 1769480 | tf_op jit(solution)/shard_map/ppermute | solution.py:21
  12.5 26.1 %collective-permute-start.1 = (f32[1152,128]{1,0:T(8,128)S(1)}, f32[1152,128]{1,0:T(8,128)S(1)}, u32[]{:S(2)}, u32[]{:S(2)}) collective-permute-start(f32[1152,128]{1,0:T(8,128)S(1)} %get-tuple-element.13.refs_0_), channel_id=1, source_target_pairs={{0,16},{4,20},{8,24},{12,28},{16,0},{20,4},{24,8},{28,12},{32,48},... | collective-permute-start | bytes 1769480 | tf_op jit(solution)/shard_map/ppermute | solution.py:21
